TPU v7x, 32 devices: a whole 2x2x4 slice. The times are simulated.
32 devices in a mesh: groups: 2 (over x), row: 16 (over z, y, core).
Axes of the slice: x: 2, y: 2, z: 4, core: 2. Of those that a mesh axis runs over, the one named last changes fastest.
Arguments:
- left_proj: bfloat16 [128, 8192], P('groups', 'row'), parts along dimension 0, may hold values from -6 to 6
- right_proj: bfloat16 [128, 8192], P('groups', 'row'), parts along dimension 0, may hold values from -6 to 6
- pair_cot: bfloat16 [512, 256, 128], P(('groups', 'row')), parts along dimension 0, may hold values from -6 to 6
- out_weight: bfloat16 [1024, 128], replicated, may hold values from -0.1875 to 0.1875
Outputs:
- grad_left: bfloat16 [128, 8192], P('groups', 'row'), parts along dimension 0
- grad_right: bfloat16 [128, 8192], P('groups', 'row'), parts along dimension 0
There are 2 independent parts, one for each index of `groups`. A program takes and returns all parts, laid end to end along the dimension named above; an argument that names none is the same for every part. Nothing has to cross between parts.
All inputs are finite; a program needn't handle non-finite values.
Results may differ from a plain program's by a relative error of at most 0.005.
Values may be sent and summed in bfloat16 or wider, within the bound.
A program may use at most 128 MiB of HBM per device.

v0:
```python
import math

import jax
import jax.numpy as jnp
from jax import lax
from jax.sharding import PartitionSpec as P

C = 32


def project_tile(slab, out_weight, n_seq):
    rows = slab.shape[0] * slab.shape[1]
    flat = slab.reshape(rows, slab.shape[2])
    prod = lax.dot_general(
        flat, out_weight, (((1,), (1,)), ((), ())), preferred_element_type=jnp.float32
    )
    return (prod / n_seq).astype(jnp.bfloat16).reshape(slab.shape[0], slab.shape[1], C, C)


def column_blocks(pair_cot, right_full, left_own, out_weight):
    n_seq = right_full.shape[0]
    own_rows = pair_cot.shape[0]
    total = pair_cot.shape[1]
    width = math.gcd(total, 256)
    n_blocks = total // width

    def block_step(carry, index):
        row_acc, partial_value = carry
        begin = index * width
        slab = lax.dynamic_slice_in_dim(pair_cot, begin, width, 1)
        right_blk = lax.dynamic_slice_in_dim(right_full, begin, width, 1)
        grad = project_tile(slab, out_weight, n_seq)
        row_acc = row_acc + jnp.einsum(
            "ijce,sje->sic", grad, right_blk, preferred_element_type=jnp.float32
        )
        piece = jnp.einsum("ijce,sic->sje", grad, left_own, preferred_element_type=jnp.float32)
        partial_value = lax.dynamic_update_slice_in_dim(partial_value, piece, begin, 1)
        return ((row_acc, partial_value), None)

    row_start = jnp.zeros((n_seq, own_rows, C), jnp.float32)
    part_start = jnp.zeros((n_seq, total, C), jnp.float32)
    (row_acc, partial_value), unused = lax.scan(
        block_step, (row_start, part_start), jnp.arange(n_blocks, dtype=jnp.int32)
    )
    return (row_acc, partial_value)


def per_device(left_proj, right_proj, pair_cot, out_weight):
    n_seq = left_proj.shape[0]
    own_rows = pair_cot.shape[0]
    total = pair_cot.shape[1]
    right_full = lax.all_gather(right_proj, "row", axis=1, tiled=True).reshape(n_seq, total, C)
    left_own = left_proj.reshape(n_seq, own_rows, C)
    row_acc, partial_sum = column_blocks(pair_cot, right_full, left_own, out_weight)
    summed = lax.psum_scatter(
        partial_sum.reshape(n_seq, total * C), "row", scatter_dimension=1, tiled=True
    )
    grad_right = summed.astype(jnp.bfloat16)
    grad_left = row_acc.reshape(n_seq, own_rows * C).astype(jnp.bfloat16)
    return (grad_left, grad_right)


def solution(mesh):
    return jax.shard_map(
        per_device,
        mesh=mesh,
        in_specs=(P("groups", "row"), P("groups", "row"), P(("groups", "row"), None, None), P()),
        out_specs=(P("groups", "row"), P("groups", "row")),
        check_vma=False,
    )
```

profile of v0, /device:TPU:0, one launch (start us, length us, event | category | flops | bytes accessed | tf_op | source)
XLA Modules:
  0.0 134.1 jit_solution(7083638522827316975)
XLA Ops:
  7.2 0.0 copy-start
  7.2 0.0 all-gather.2.cloned.1.call-start
  7.2 0.7 all-gather.2.cloned.1.call-update
  7.9 0.0 reduce-scatter.2.cloned.1.call-start
  8.0 0.4 copy-done
  8.4 6.5 %multiply_convert_fusion = bf16[4096,1024]{1,0:T(8,128)(2,1)} fusion(bf16[4096,128]{1,0:T(8,128)(2,1)S(1)} %bitcast.28, bf16[1024,128]{1,0:T(8,128)(2,1)} %param.7), kind=kOutput, calls=%fused_computation | convolution fusion | flops 1082130432 | bytes 9699328 | tf_op jit(solution)/shard_map/while/body/eval_jaxpr/dot_general | solution.py:14
  14.9 11.7 %copy.10 = bf16[4096,1024]{0,1:T(8,128)(2,1)} copy(bf16[4096,1024]{1,0:T(8,128)(2,1)} %multiply_convert_fusion) | data formatting | bytes 16777216 | tf_op jit(solution)/shard_map/while/body/eval_jaxpr/convert_element_type | solution.py:17
  26.6 0.0 copy-start.1
  26.6 9.8 %copy.23 = bf16[128,8,16,256]{3,2,1,0:T(8,128)(2,1)} copy(bf16[128,8,16,256]{3,1,2,0:T(8,128)(2,1)} %bitcast.31) | data formatting | bytes 16777216
  36.3 0.0 copy-done.1
  36.3 0.1 copy.14
  36.5 5.0 %convolution_bitcast_fusion = f32[64,256,32]{1,0,2:T(8,128)S(1)} fusion(bf16[16,256,32,32]{1,0,3,2:T(8,128)(2,1)} %bitcast.29, bf16[64,16,32,1]{0,2,1,3:T(8,128)(2,1)S(1)} %bitcast.35), kind=kOutput, calls=%fused_computation.1 | convolution fusion | flops 536870912 | bytes 10551296 | tf_op jit(solution)/shard_map/while/body/eval_jaxpr/ijce,sic->sje/dot_general | solution.py:36
  41.5 4.5 %copy.16 = f32[64,256,32]{0,2,1:T(8,128)} copy(f32[64,256,32]{1,0,2:T(8,128)S(1)} %convolution_bitcast_fusion) | data formatting | bytes 4194304 | tf_op jit(solution)/shard_map/while/body/eval_jaxpr/ijce,sic->sje/dot_general | solution.py:36
  46.0 0.0 reduce-scatter.2.cloned.1.call-update
  46.0 3.7 %all-gather.2.cloned.1.call-done = bf16[64,8192]{1,0:T(8,128)(2,1)} async-done(((bf16[64,512]{1,0:T(8,128)(2,1)}), bf16[64,8192]{1,0:T(8,128)(2,1)}) %all-gather.2.cloned.1.call-update) | async-done | bytes 1048592 | tf_op jit(solution)/shard_map/all_gather | solution.py:52
  49.7 2.0 %copy.11 = bf16[64,8192]{0,1:T(8,128)(2,1)S(1)} copy(bf16[64,8192]{1,0:T(8,128)(2,1)} %all-gather.2.cloned.1.call-done) | data formatting | bytes 2097152 | tf_op jit(solution)/shard_map/all_gather | solution.py:52
  51.7 2.5 %copy.13 = bf16[64,256,32]{1,0,2:T(8,128)(2,1)} copy(bf16[64,256,32]{0,2,1:T(8,128)(2,1)S(1)} %bitcast.33) | data formatting | bytes 2097152 | tf_op jit(solution)/shard_map/reshape | solution.py:52
  54.3 5.9 %fusion = bf16[16,32,64,1]{2,0,3,1:T(8,128)(2,1)S(1)} fusion(bf16[16,256,32,32]{1,0,3,2:T(8,128)(2,1)} %bitcast.30, bf16[64,256,32]{1,0,2:T(8,128)(2,1)} %copy.13), kind=kOutput, calls=%fused_computation.2 | convolution fusion | flops 536870912 | bytes 9502720 | tf_op jit(solution)/shard_map/while/body/eval_jaxpr/ijce,sje->sic/dot_general | solution.py:33
  60.2 0.7 copy.17
  60.9 64.6 %reduce-scatter.2.cloned.1.call-done = f32[64,512]{0,1:T(8,128)} async-done(((f32[64,8192]{0,1:T(8,128)}), f32[64,512]{0,1:T(8,128)}) %reduce-scatter.2.cloned.1.call-update) | async-done | bytes 131088 | tf_op jit(solution)/shard_map/reduce_scatter | solution.py:55
  125.6 1.0 convert_element_type.20
  126.5 0.7 copy.18
  (1 shorter events, 0.0 us)
Async XLA Ops:
  7.2 1.2 copy-start
  7.2 42.5 %all-gather.2.cloned.1.call-start = ((), (), s32[]{:S(2)}) async-start(), calls=%async_computation.1 | async-start | bytes 1114112 | tf_op jit(solution)/shard_map/all_gather | solution.py:52
  7.9 117.6 %reduce-scatter.2.cloned.1.call-start = ((), (), s32[]{:S(2)}) async-start(), calls=%async_computation.2 | async-start | bytes 4456448 | tf_op jit(solution)/shard_map/reduce_scatter | solution.py:55
  26.6 9.8 %copy-start.1 = (bf16[64,512]{1,0:T(8,128)(2,1)S(1)}, bf16[64,512]{1,0:T(8,128)(2,1)}, u32[]{:S(2)}) copy-start(bf16[64,512]{1,0:T(8,128)(2,1)} %param.4) | copy-start | bytes 196612
Sparse Core Ops, SparseCore 0:
  10.2 39.4 all-gather.1
  53.6 71.9 reduce-scatter.1
where the time goes:
time: 135 us; the launch traced here: 134 us
  waiting for transfers between devices  69 us (51%)
  local copies, waits for them, and re-layouts  32.5 us (24%)
  matrix products  17.5 us (13%)
  between operations  14.1 us (10%)
    reduce_scatter x1, waiting for transfers between devices, per_device(): lax.psum_scatter(partial_sum.reshape(n_seq, total * C), 'row', scatter_di...  64.6 us
    unnamed x8, local copies, waits for them, and re-layouts  11.8 us
    convert_element_type x1, local copies, waits for them, and re-layouts, project_tile(): (prod / n_seq).astype(jnp.bfloat16)  11.7 us
    dot_general x1, matrix products, project_tile(): lax.dot_general(flat, out_weight, (((1,), (1,)), ((), ())), preferred_ele...  6.52 us
    dot_general x1, matrix products, block_step(): jnp.einsum('ijce,sje->sic', grad, right_blk, preferred_element_type=jnp.f...  5.91 us
    dot_general x1, matrix products, block_step(): jnp.einsum('ijce,sic->sje', grad, left_own, preferred_element_type=jnp.fl...  5.02 us
    dot_general x1, local copies, waits for them, and re-layouts, block_step(): jnp.einsum('ijce,sic->sje', grad, left_own, preferred_element_type=jnp.fl...  4.48 us
    all_gather x1, waiting for transfers between devices, per_device(): lax.all_gather(right_proj, 'row', axis=1, tiled=True)  3.71 us
  transfers between devices with their start and end apart: 2, of which 2 were waited for; matrix products, arithmetic and copies ran while one was open for 36% of the time, Pallas kernels for 0%

commit v1 on v0

v1 whole, which is shorter than its diff:
```python
import functools

import jax
import jax.numpy as jnp
from jax import lax
from jax.experimental import pallas as pl
from jax.experimental.pallas import tpu as pltpu
from jax.sharding import PartitionSpec as P

C = 32
CORES = 2
COLS = 2
HALF = C // 2
GROUPS = 4
MESH = pl.DeviceIdType.MESH
F32 = jnp.float32
BF16 = jnp.bfloat16


def kernel(
    depth, n_seq, block,
    left_ref, right_ref, pair_ref, weight_ref,
    out_left, out_right,
    pair_own, pair_sib, left_sib, weight_f32, weight_perm, grad, rows_f32,
    gathered, right_all, column_sum, y_send, y_recv, z_send, z_recv, total,
    left_acc, left_send, left_recv,
    load_sem, sib_send, sib_recv, agz_send, agz_recv, agy_send, agy_recv,
    rsy_send, rsy_recv, rsz_send, rsz_recv,
):
    me = lax.axis_index("row")
    core = lax.rem(me, CORES)
    col = lax.rem(me // CORES, COLS)
    z = me // (CORES * COLS)
    sibling = me + 1 - 2 * core
    across = me + CORES * (1 - 2 * col)
    span = depth * block
    width = COLS * span
    chans = block * C
    lanes = 2 * n_seq
    per_group = HALF // GROUPS
    group_lanes = per_group * lanes

    def z_peer(step):
        return lax.rem(z + step, depth)

    def at_z(other):
        return other * (CORES * COLS) + lax.rem(me, CORES * COLS)

    def send(src, dst, s_sem, r_sem, target):
        return pltpu.make_async_remote_copy(
            src_ref=src, dst_ref=dst, send_sem=s_sem, recv_sem=r_sem,
            device_id={"row": target}, device_id_type=MESH,
        )

    barrier = pltpu.get_barrier_semaphore()
    for target in [sibling, across] + [at_z(z_peer(d)) for d in range(1, depth)]:
        pl.semaphore_signal(barrier, inc=1, device_id={"row": target}, device_id_type=MESH)

    loads = []
    for rel in range(COLS):
        which = col if rel == 0 else 1 - col
        loads.append(pltpu.make_async_copy(
            pair_ref.at[:, :, which, core], pair_own.at[:, rel], load_sem.at[rel]))
        loads[-1].start()

    wide = right_ref[...].astype(F32)
    rows_f32[...] = jnp.concatenate([wide, wide], axis=0).T
    low = lax.broadcasted_iota(jnp.int32, (block, lanes), 1) < n_seq
    for ep in range(HALF):
        even = rows_f32[pl.ds(2 * ep, block, stride=C), :]
        odd = rows_f32[pl.ds(2 * ep + 1, block, stride=C), :]
        gathered[ep, 0, z] = jnp.where(low, even, odd).astype(BF16)

    pl.semaphore_wait(barrier, depth + 1)

    sib = []
    for rel in range(COLS):
        which = col if rel == 0 else 1 - col
        sib.append(send(pair_ref.at[:, :, which, 1 - core], pair_sib.at[:, rel],
                        sib_send.at[rel], sib_recv.at[rel], sibling))
    sib.append(send(left_ref, left_sib, sib_send.at[2], sib_recv.at[2], sibling))
    gather_z = [
        send(gathered.at[:, 0, z], gathered.at[:, 0, z], agz_send.at[d - 1], agz_recv.at[d - 1],
             at_z(z_peer(d)))
        for d in range(1, depth)
    ]
    gather_y = []
    for d in range(depth):
        other = z if d == 0 else lax.rem(z + depth - d, depth)
        gather_y.append(send(gathered.at[:, 0, other], gathered.at[:, 1, other],
                             agy_send.at[d], agy_recv.at[d], across))
    for copy in gather_z:
        copy.start()
    for copy in sib:
        copy.start()
    gather_y[0].start()

    weight_f32[...] = weight_ref[...].astype(F32)
    for e in range(C):
        weight_perm[e * C:(e + 1) * C, :] = weight_f32[pl.ds(e, C, stride=C), :].astype(BF16)

    def project(pair, first):
        def step(t, carry):
            slab = pair[pl.ds(2 * t, 2)].reshape(2 * width, -1)
            res = lax.dot_general(weight_perm[...], slab, (((1,), (1,)), ((), ())),
                                  preferred_element_type=F32).astype(BF16)
            for k in range(2):
                row = pl.multiple_of(first + (2 * t + k) * C, C)
                for e in range(C):
                    grad[pl.ds(row, C), e * width:(e + 1) * width] = (
                        res[e * C:(e + 1) * C, k * width:(k + 1) * width])
            return carry

        lax.fori_loop(0, block // 2, step, 0)

    for copy in loads:
        copy.wait()
    project(pair_own, 0)
    for d in range(1, depth):
        gather_z[d - 1].wait_recv()
        gather_y[d].start()
    for copy in sib:
        copy.wait_recv()
    project(pair_sib, chans)

    reduce_y = [send(y_send.at[g], y_recv.at[g], rsy_send.at[g], rsy_recv.at[g], across)
                for g in range(GROUPS)]
    reduce_z = [
        [send(z_send.at[g, z_peer(d)], z_recv.at[g, d - 1],
              rsz_send.at[g, d - 1], rsz_recv.at[g, d - 1], at_z(z_peer(d)))
         for d in range(1, depth)]
        for g in range(GROUPS)
    ]

    def columns(g):
        for q in range(per_group):
            ep = g * per_group + q
            part = slice(2 * ep * width, 2 * (ep + 1) * width)
            res = jnp.dot(left_ref[...], grad[:chans, part], preferred_element_type=F32)
            res += jnp.dot(left_sib[...], grad[chans:, part], preferred_element_type=F32)
            turned = jnp.concatenate([res[:, :width], res[:, width:]], axis=0).T
            where = slice(q * lanes, (q + 1) * lanes)
            column_sum[g, :, where] = turned[:span]
            y_send[g, :, where] = turned[span:].astype(BF16)
        reduce_y[g].start()

    def second(g):
        reduce_y[g].wait_recv()
        column_sum[g] += y_recv[g].astype(F32)
        for k in range(depth):
            z_send[g, k] = column_sum[g, k * block:(k + 1) * block, :].astype(BF16)
        for copy in reduce_z[g]:
            copy.start()

    def rows(first):
        left_acc[...] = jnp.zeros_like(left_acc)

        def step(ep, carry):
            at = pl.multiple_of(ep * 2 * width, 2 * width)
            left_acc[...] += jnp.dot(grad[first:first + chans, pl.ds(at, 2 * width)],
                                     right_all[pl.ds(at, 2 * width), :],
                                     preferred_element_type=F32)
            return carry

        lax.fori_loop(0, HALF, step, 0)
        turned = left_acc[...].T
        return turned[:n_seq] + turned[n_seq:]

    columns(0)
    columns(1)
    columns(2)
    second(0)
    columns(3)
    second(1)

    for copy in gather_y:
        copy.wait_recv()
    upper = lax.broadcasted_iota(jnp.int32, (width, lanes), 1) >= n_seq
    mask_odd = upper.astype(F32).astype(BF16)
    mask_even = (1.0 - upper.astype(F32)).astype(BF16)
    for ep in range(HALF):
        piece = gathered[ep].reshape(width, lanes)
        right_all[2 * ep * width:(2 * ep + 1) * width, :] = piece * mask_even
        right_all[(2 * ep + 1) * width:(2 * ep + 2) * width, :] = piece * mask_odd

    second(2)
    left_send[...] = rows(chans)
    exchange = send(left_send, left_recv, sib_send.at[3], sib_recv.at[3], sibling)
    exchange.start()
    second(3)
    mine = rows(0)
    exchange.wait_recv()
    out_left[...] = ((mine + left_recv[...]) * (1.0 / n_seq)).astype(BF16)

    for g in range(GROUPS):
        acc = column_sum[g, pl.ds(pl.multiple_of(z * block, block), block), :]
        for d in range(1, depth):
            reduce_z[g][d - 1].wait_recv()
            acc += z_recv[g, d - 1].astype(F32)
        for q in range(per_group):
            ep = g * per_group + q
            tile = acc[:, q * lanes:(q + 1) * lanes] * (1.0 / n_seq)
            rows_f32[pl.ds(2 * ep, block, stride=C), :] = tile
            rows_f32[pl.ds(2 * ep + 1, block, stride=C), :] = pltpu.roll(tile, n_seq, 1)
    out_right[...] = rows_f32[...].T[:n_seq].astype(BF16)

    for copy in sib + gather_z + gather_y + reduce_y + [exchange]:
        copy.wait_send()
    for group in reduce_z:
        for copy in group:
            copy.wait_send()


def per_device(n_row, left_proj, right_proj, pair_cot, out_weight):
    n_seq = left_proj.shape[0]
    block, total, p_size = pair_cot.shape
    depth = n_row // (CORES * COLS)
    span = depth * block
    width = COLS * span
    chans = block * C
    lanes = 2 * n_seq
    group_lanes = HALF // GROUPS * lanes
    pair = pair_cot.reshape(block, depth, COLS, CORES, block, p_size)
    vmem = pl.BlockSpec(memory_space=pltpu.VMEM)
    dma = pltpu.SemaphoreType.DMA
    flops = 2 * block * total * C * C * (p_size + 2 * n_seq)
    return pl.pallas_call(
        functools.partial(kernel, depth, n_seq, block),
        out_shape=[jax.ShapeDtypeStruct((n_seq, chans), BF16)] * 2,
        in_specs=[vmem, vmem, pl.BlockSpec(memory_space=pl.ANY), vmem],
        out_specs=[vmem, vmem],
        scratch_shapes=[
            pltpu.VMEM((block, COLS, depth, block, p_size), BF16),
            pltpu.VMEM((block, COLS, depth, block, p_size), BF16),
            pltpu.VMEM((n_seq, chans), BF16),
            pltpu.VMEM((C * C, p_size), F32),
            pltpu.VMEM((C * C, p_size), BF16),
            pltpu.VMEM((2 * chans, C * width), BF16),
            pltpu.VMEM((chans, lanes), F32),
            pltpu.VMEM((HALF, COLS, depth, block, lanes), BF16),
            pltpu.VMEM((C * width, lanes), BF16),
            pltpu.VMEM((GROUPS, span, group_lanes), F32),
            pltpu.VMEM((GROUPS, span, group_lanes), BF16),
            pltpu.VMEM((GROUPS, span, group_lanes), BF16),
            pltpu.VMEM((GROUPS, depth, block, group_lanes), BF16),
            pltpu.VMEM((GROUPS, depth - 1, block, group_lanes), BF16),
            pltpu.VMEM((8, 128), F32),
            pltpu.VMEM((chans, lanes), F32),
            pltpu.VMEM((n_seq, chans), F32),
            pltpu.VMEM((n_seq, chans), F32),
            dma((COLS,)),
            dma((4,)), dma((4,)),
            dma((depth - 1,)), dma((depth - 1,)),
            dma((depth,)), dma((depth,)),
            dma((GROUPS,)), dma((GROUPS,)),
            dma((GROUPS, depth - 1)), dma((GROUPS, depth - 1)),
        ],
        compiler_params=pltpu.CompilerParams(
            collective_id=0, has_side_effects=True, vmem_limit_bytes=60 * 1024 * 1024
        ),
        cost_estimate=pl.CostEstimate(
            flops=flops, bytes_accessed=4 * pair_cot.size, transcendentals=0
        ),
    )(left_proj, right_proj, pair, out_weight)


def solution(mesh):
    return jax.shard_map(
        functools.partial(per_device, mesh.shape["row"]),
        mesh=mesh,
        in_specs=(P("groups", "row"), P("groups", "row"), P(("groups", "row"), None, None), P()),
        out_specs=(P("groups", "row"), P("groups", "row")),
        check_vma=False,
    )
```

time: 135 us -> 34.4 us (0.25)
  waiting for transfers between devices: 69 us -> 0 us
  Pallas kernels: 0 us -> 31.4 us
  local copies, waits for them, and re-layouts: 32.5 us -> 2.14 us
  matrix products: 17.5 us -> 0 us
  between operations: 14.1 us -> 0.65 us
    reduce_scatter x1 -> x0, waiting for transfers between devices: 64.6 us -> none  [per_device(): lax.psum_scatter(partial_sum.reshape(n_seq, total * C), 'row', scatter_di...]
    pallas_call x0 -> x1, Pallas kernels: none -> 31.4 us  [per_device(): pl.pallas_call(functools.partial(kernel, depth, n_seq, block), out_shape=...]
    dot_general x3 -> x0, matrix products: 17.5 us -> none  [the longest x1 6.52 us: project_tile(): lax.dot_general(flat, out_weight, (((1,), (1,)), ((), ())), preferred_ele...]
    convert_element_type x1 -> x0, local copies, waits for them, and re-layouts: 11.7 us -> none  [project_tile(): (prod / n_seq).astype(jnp.bfloat16)]
    unnamed x8 -> x4, local copies, waits for them, and re-layouts: 11.8 us -> 2.14 us
    dot_general x2 -> x0, local copies, waits for them, and re-layouts: 4.51 us -> none  [the longest x1 4.48 us: block_step(): jnp.einsum('ijce,sic->sje', grad, left_own, preferred_element_type=jnp.fl...]
    all_gather x1 -> x0, waiting for transfers between devices: 3.71 us -> none  [per_device(): lax.all_gather(right_proj, 'row', axis=1, tiled=True)]
    reshape x1 -> x0, local copies, waits for them, and re-layouts: 2.52 us -> none  [per_device(): lax.all_gather(right_proj, 'row', axis=1, tiled=True)]
  transfers between devices with their start and end apart: 2 -> 0, of which waited for: 2 -> 0; matrix products, arithmetic and copies ran while one was open for 36% -> 0% of each run, Pallas kernels for 0% -> 0%
where the time goes in v1:
time: 34.4 us; the launch traced here: 34.2 us
  Pallas kernels  31.4 us (91%)
  local copies, waits for them, and re-layouts  2.14 us (6%)
  between operations  0.65 us (2%)
    pallas_call x1, Pallas kernels, per_device(): pl.pallas_call(functools.partial(kernel, depth, n_seq, block), out_shape=...  31.4 us
    unnamed x4, local copies, waits for them, and re-layouts  2.14 us

profile of v1, /device:TPU:0, one launch (start us, length us, event | category | flops | bytes accessed | tf_op | source)
XLA Modules:
  0.0 34.2 jit_solution(6541320027158219408)
XLA Ops:
  0.6 31.4 %shard_map.59 = (bf16[64,512]{1,0:T(8,128)(2,1)}, bf16[64,512]{1,0:T(8,128)(2,1)}) custom-call(bf16[64,512]{1,0:T(8,128)(2,1)} %left_ref.1, bf16[64,512]{1,0:T(8,128)(2,1)} %right_ref.1, bf16[16,4,2,2,16,128]{5,4,3,2,1,0:T(8,128)(2,1)} %bitcast.1, bf16[1024,128]{1,0:T(8,128)(2,1)} %weight_ref.1), custom_call_target="tpu_custom_call" | custom-call | flops 2147483648 | bytes 2097152 | tf_op jit(solution)/shard_map/pallas_call | solution.py:227
  32.1 0.0 copy-start
  32.1 1.5 %copy.8 = bf16[64,512]{1,0:T(8,128)(2,1)} copy(bf16[64,512]{1,0:T(8,128)(2,1)} %get-tuple-element.4) | data formatting | bytes 131072
  33.6 0.0 copy-done
  33.6 0.6 %copy.9 = bf16[64,512]{1,0:T(8,128)(2,1)} copy(bf16[64,512]{1,0:T(8,128)(2,1)S(1)} %copy-done) | data formatting | bytes 131072
Async XLA Ops:
  32.1 1.5 %copy-start = (bf16[64,512]{1,0:T(8,128)(2,1)S(1)}, bf16[64,512]{1,0:T(8,128)(2,1)}, u32[]{:S(2)}) copy-start(bf16[64,512]{1,0:T(8,128)(2,1)} %get-tuple-element.5) | copy-start | bytes 196612

commit v2 on v1

--- a/solution.py
+++ b/solution.py
@@ -20,10 +20,10 @@
 def kernel(
     depth, n_seq, block,
     left_ref, right_ref, pair_ref, weight_ref,
-    out_left, out_right,
+    out,
     pair_own, pair_sib, left_sib, weight_f32, weight_perm, grad, rows_f32,
-    gathered, right_all, column_sum, y_send, y_recv, z_send, z_recv, total,
-    left_acc, left_send, left_recv,
+    gathered, right_all, column_sum, y_send, y_recv, z_send, z_recv,
+    left_send, left_recv,
     load_sem, sib_send, sib_recv, agz_send, agz_recv, agy_send, agy_recv,
     rsy_send, rsy_recv, rsz_send, rsz_recv,
 ):
@@ -99,29 +99,24 @@
     for e in range(C):
         weight_perm[e * C:(e + 1) * C, :] = weight_f32[pl.ds(e, C, stride=C), :].astype(BF16)
 
-    def project(pair, first):
+    rows_g = C // GROUPS * C
+
+    def project(g, pair, first):
+        taps = weight_perm[g * rows_g:(g + 1) * rows_g, :]
+
         def step(t, carry):
             slab = pair[pl.ds(2 * t, 2)].reshape(2 * width, -1)
-            res = lax.dot_general(weight_perm[...], slab, (((1,), (1,)), ((), ())),
+            res = lax.dot_general(taps, slab, (((1,), (1,)), ((), ())),
                                   preferred_element_type=F32).astype(BF16)
             for k in range(2):
                 row = pl.multiple_of(first + (2 * t + k) * C, C)
-                for e in range(C):
+                for q in range(C // GROUPS):
+                    e = g * (C // GROUPS) + q
                     grad[pl.ds(row, C), e * width:(e + 1) * width] = (
-                        res[e * C:(e + 1) * C, k * width:(k + 1) * width])
+                        res[q * C:(q + 1) * C, k * width:(k + 1) * width])
             return carry
 
-        lax.fori_loop(0, block // 2, step, 0)
-
-    for copy in loads:
-        copy.wait()
-    project(pair_own, 0)
-    for d in range(1, depth):
-        gather_z[d - 1].wait_recv()
-        gather_y[d].start()
-    for copy in sib:
-        copy.wait_recv()
-    project(pair_sib, chans)
+        lax.fori_loop(0, block // 2, step, 0, unroll=4)
 
     reduce_y = [send(y_send.at[g], y_recv.at[g], rsy_send.at[g], rsy_recv.at[g], across)
                 for g in range(GROUPS)]
@@ -133,12 +128,13 @@
     ]
 
     def columns(g):
+        part = slice(g * per_group * 2 * width, (g + 1) * per_group * 2 * width)
+        res = jnp.dot(left_ref[...], grad[:chans, part], preferred_element_type=F32)
+        res += jnp.dot(left_sib[...], grad[chans:, part], preferred_element_type=F32)
         for q in range(per_group):
-            ep = g * per_group + q
-            part = slice(2 * ep * width, 2 * (ep + 1) * width)
-            res = jnp.dot(left_ref[...], grad[:chans, part], preferred_element_type=F32)
-            res += jnp.dot(left_sib[...], grad[chans:, part], preferred_element_type=F32)
-            turned = jnp.concatenate([res[:, :width], res[:, width:]], axis=0).T
+            at = 2 * q * width
+            turned = jnp.concatenate(
+                [res[:, at:at + width], res[:, at + width:at + 2 * width]], axis=0).T
             where = slice(q * lanes, (q + 1) * lanes)
             column_sum[g, :, where] = turned[:span]
             y_send[g, :, where] = turned[span:].astype(BF16)
@@ -153,25 +149,30 @@
             copy.start()
 
     def rows(first):
-        left_acc[...] = jnp.zeros_like(left_acc)
-
-        def step(ep, carry):
-            at = pl.multiple_of(ep * 2 * width, 2 * width)
-            left_acc[...] += jnp.dot(grad[first:first + chans, pl.ds(at, 2 * width)],
-                                     right_all[pl.ds(at, 2 * width), :],
-                                     preferred_element_type=F32)
-            return carry
-
-        lax.fori_loop(0, HALF, step, 0)
-        turned = left_acc[...].T
+        part = per_group * 2 * width
+        acc = None
+        for g in range(GROUPS):
+            term = jnp.dot(grad[first:first + chans, g * part:(g + 1) * part],
+                           right_all[g * part:(g + 1) * part, :], preferred_element_type=F32)
+            acc = term if acc is None else acc + term
+        turned = acc.T
         return turned[:n_seq] + turned[n_seq:]
 
-    columns(0)
-    columns(1)
-    columns(2)
-    second(0)
-    columns(3)
-    second(1)
+    for copy in loads:
+        copy.wait()
+    for g in range(GROUPS):
+        project(g, pair_own, 0)
+        if g == 0:
+            for copy in sib:
+                copy.wait_recv()
+        project(g, pair_sib, chans)
+        for d in range(1, depth):
+            if (d - 1) * (GROUPS - 1) // (depth - 1) == g - 1:
+                gather_z[d - 1].wait_recv()
+                gather_y[d].start()
+        columns(g)
+        if g >= 2:
+            second(g - 2)
 
     for copy in gather_y:
         copy.wait_recv()
@@ -190,7 +191,7 @@
     second(3)
     mine = rows(0)
     exchange.wait_recv()
-    out_left[...] = ((mine + left_recv[...]) * (1.0 / n_seq)).astype(BF16)
+    out[0] = ((mine + left_recv[...]) * (1.0 / n_seq)).astype(BF16)
 
     for g in range(GROUPS):
         acc = column_sum[g, pl.ds(pl.multiple_of(z * block, block), block), :]
@@ -202,7 +203,7 @@
             tile = acc[:, q * lanes:(q + 1) * lanes] * (1.0 / n_seq)
             rows_f32[pl.ds(2 * ep, block, stride=C), :] = tile
             rows_f32[pl.ds(2 * ep + 1, block, stride=C), :] = pltpu.roll(tile, n_seq, 1)
-    out_right[...] = rows_f32[...].T[:n_seq].astype(BF16)
+    out[1] = rows_f32[...].T[:n_seq].astype(BF16)
 
     for copy in sib + gather_z + gather_y + reduce_y + [exchange]:
         copy.wait_send()
@@ -224,11 +225,11 @@
     vmem = pl.BlockSpec(memory_space=pltpu.VMEM)
     dma = pltpu.SemaphoreType.DMA
     flops = 2 * block * total * C * C * (p_size + 2 * n_seq)
-    return pl.pallas_call(
+    sums = pl.pallas_call(
         functools.partial(kernel, depth, n_seq, block),
-        out_shape=[jax.ShapeDtypeStruct((n_seq, chans), BF16)] * 2,
+        out_shape=jax.ShapeDtypeStruct((2, n_seq, chans), BF16),
         in_specs=[vmem, vmem, pl.BlockSpec(memory_space=pl.ANY), vmem],
-        out_specs=[vmem, vmem],
+        out_specs=vmem,
         scratch_shapes=[
             pltpu.VMEM((block, COLS, depth, block, p_size), BF16),
             pltpu.VMEM((block, COLS, depth, block, p_size), BF16),
@@ -244,8 +245,6 @@
             pltpu.VMEM((GROUPS, span, group_lanes), BF16),
             pltpu.VMEM((GROUPS, depth, block, group_lanes), BF16),
             pltpu.VMEM((GROUPS, depth - 1, block, group_lanes), BF16),
-            pltpu.VMEM((8, 128), F32),
-            pltpu.VMEM((chans, lanes), F32),
             pltpu.VMEM((n_seq, chans), F32),
             pltpu.VMEM((n_seq, chans), F32),
             dma((COLS,)),
@@ -262,6 +261,7 @@
             flops=flops, bytes_accessed=4 * pair_cot.size, transcendentals=0
         ),
     )(left_proj, right_proj, pair, out_weight)
+    return (sums[0], sums[1])
 
 
 def solution(mesh):

time: 34.4 us -> 29.9 us (0.87)
  Pallas kernels: 31.4 us -> 27.5 us
  local copies, waits for them, and re-layouts: 2.14 us -> 1.53 us
    pallas_call x1, Pallas kernels: 31.4 us -> 27.5 us  [per_device(): pl.pallas_call(functools.partial(kernel, depth, n_seq, block), out_shape=...]
    unnamed x4 -> x0, local copies, waits for them, and re-layouts: 2.14 us -> none
    squeeze x0 -> x1, local copies, waits for them, and re-layouts: none -> 1.53 us  [per_device(): return (sums[0], sums[1])]
where the time goes in v2:
time: 29.9 us; the launch traced here: 29.7 us
  Pallas kernels  27.5 us (92%)
  local copies, waits for them, and re-layouts  1.53 us (5%)
  between operations  0.64 us (2%)
    pallas_call x1, Pallas kernels, per_device(): pl.pallas_call(functools.partial(kernel, depth, n_seq, block), out_shape=...  27.5 us
    squeeze x1, local copies, waits for them, and re-layouts, per_device(): return (sums[0], sums[1])  1.53 us

profile of v2, /device:TPU:0, one launch (start us, length us, event | category | flops | bytes accessed | tf_op | source)
XLA Modules:
  0.0 29.7 jit_solution(2886367011419364)
XLA Ops:
  0.6 27.5 %shard_map.59 = bf16[2,64,512]{2,1,0:T(8,128)(2,1)} custom-call(bf16[64,512]{1,0:T(8,128)(2,1)} %left_ref.1, bf16[64,512]{1,0:T(8,128)(2,1)} %right_ref.1, bf16[16,4,2,2,16,128]{5,4,3,2,1,0:T(8,128)(2,1)} %bitcast.5, bf16[1024,128]{1,0:T(8,128)(2,1)} %weight_ref.1), custom_call_target="tpu_custom_call" | custom-call | flops 2147483648 | bytes 2097152 | tf_op jit(solution)/shard_map/pallas_call | solution.py:228
  28.2 1.5 %slice_bitcast_fusion = (bf16[64,512]{1,0:T(8,128)(2,1)}, bf16[64,512]{1,0:T(8,128)(2,1)}) fusion(bf16[2,64,512]{2,1,0:T(8,128)(2,1)} %shard_map.59), kind=kLoop, calls=%fused_computation | loop fusion | bytes 262144 | tf_op jit(solution)/shard_map/squeeze | solution.py:264

commit v3 on v2

--- a/solution.py
+++ b/solution.py
@@ -1,4 +1,5 @@
 import functools
+import math
 
 import jax
 import jax.numpy as jnp
@@ -11,7 +12,7 @@
 CORES = 2
 COLS = 2
 HALF = C // 2
-GROUPS = 4
+GROUPS = 2
 MESH = pl.DeviceIdType.MESH
 F32 = jnp.float32
 BF16 = jnp.bfloat16
@@ -116,7 +117,7 @@
                         res[q * C:(q + 1) * C, k * width:(k + 1) * width])
             return carry
 
-        lax.fori_loop(0, block // 2, step, 0, unroll=4)
+        lax.fori_loop(0, block // 2, step, 0, unroll=2)
 
     reduce_y = [send(y_send.at[g], y_recv.at[g], rsy_send.at[g], rsy_recv.at[g], across)
                 for g in range(GROUPS)]
@@ -171,8 +172,6 @@
                 gather_z[d - 1].wait_recv()
                 gather_y[d].start()
         columns(g)
-        if g >= 2:
-            second(g - 2)
 
     for copy in gather_y:
         copy.wait_recv()
@@ -184,11 +183,12 @@
         right_all[2 * ep * width:(2 * ep + 1) * width, :] = piece * mask_even
         right_all[(2 * ep + 1) * width:(2 * ep + 2) * width, :] = piece * mask_odd
 
-    second(2)
+    for g in range(GROUPS - 1):
+        second(g)
     left_send[...] = rows(chans)
     exchange = send(left_send, left_recv, sib_send.at[3], sib_recv.at[3], sibling)
     exchange.start()
-    second(3)
+    second(GROUPS - 1)
     mine = rows(0)
     exchange.wait_recv()
     out[0] = ((mine + left_recv[...]) * (1.0 / n_seq)).astype(BF16)
@@ -225,37 +225,41 @@
     vmem = pl.BlockSpec(memory_space=pltpu.VMEM)
     dma = pltpu.SemaphoreType.DMA
     flops = 2 * block * total * C * C * (p_size + 2 * n_seq)
+    scratch = [
+        pltpu.VMEM((block, COLS, depth, block, p_size), BF16),
+        pltpu.VMEM((block, COLS, depth, block, p_size), BF16),
+        pltpu.VMEM((n_seq, chans), BF16),
+        pltpu.VMEM((C * C, p_size), F32),
+        pltpu.VMEM((C * C, p_size), BF16),
+        pltpu.VMEM((2 * chans, C * width), BF16),
+        pltpu.VMEM((chans, lanes), F32),
+        pltpu.VMEM((HALF, COLS, depth, block, lanes), BF16),
+        pltpu.VMEM((C * width, lanes), BF16),
+        pltpu.VMEM((GROUPS, span, group_lanes), F32),
+        pltpu.VMEM((GROUPS, span, group_lanes), BF16),
+        pltpu.VMEM((GROUPS, span, group_lanes), BF16),
+        pltpu.VMEM((GROUPS, depth, block, group_lanes), BF16),
+        pltpu.VMEM((GROUPS, depth - 1, block, group_lanes), BF16),
+        pltpu.VMEM((n_seq, chans), F32),
+        pltpu.VMEM((n_seq, chans), F32),
+        dma((COLS,)),
+        dma((4,)), dma((4,)),
+        dma((depth - 1,)), dma((depth - 1,)),
+        dma((depth,)), dma((depth,)),
+        dma((GROUPS,)), dma((GROUPS,)),
+        dma((GROUPS, depth - 1)), dma((GROUPS, depth - 1)),
+    ]
+    held = sum(2 * math.prod(b.shape) if b.dtype == BF16 else 4 * math.prod(b.shape)
+               for b in scratch if b.dtype in (BF16, F32))
+    held += 2 * 2 * (left_proj.size * 4 + out_weight.size)
     sums = pl.pallas_call(
         functools.partial(kernel, depth, n_seq, block),
         out_shape=jax.ShapeDtypeStruct((2, n_seq, chans), BF16),
-        in_specs=[vmem, vmem, pl.BlockSpec(memory_space=pl.ANY), vmem],
+        in_specs=[vmem, vmem, pl.BlockSpec(memory_space=pltpu.HBM), vmem],
         out_specs=vmem,
-        scratch_shapes=[
-            pltpu.VMEM((block, COLS, depth, block, p_size), BF16),
-            pltpu.VMEM((block, COLS, depth, block, p_size), BF16),
-            pltpu.VMEM((n_seq, chans), BF16),
-            pltpu.VMEM((C * C, p_size), F32),
-            pltpu.VMEM((C * C, p_size), BF16),
-            pltpu.VMEM((2 * chans, C * width), BF16),
-            pltpu.VMEM((chans, lanes), F32),
-            pltpu.VMEM((HALF, COLS, depth, block, lanes), BF16),
-            pltpu.VMEM((C * width, lanes), BF16),
-            pltpu.VMEM((GROUPS, span, group_lanes), F32),
-            pltpu.VMEM((GROUPS, span, group_lanes), BF16),
-            pltpu.VMEM((GROUPS, span, group_lanes), BF16),
-            pltpu.VMEM((GROUPS, depth, block, group_lanes), BF16),
-            pltpu.VMEM((GROUPS, depth - 1, block, group_lanes), BF16),
-            pltpu.VMEM((n_seq, chans), F32),
-            pltpu.VMEM((n_seq, chans), F32),
-            dma((COLS,)),
-            dma((4,)), dma((4,)),
-            dma((depth - 1,)), dma((depth - 1,)),
-            dma((depth,)), dma((depth,)),
-            dma((GROUPS,)), dma((GROUPS,)),
-            dma((GROUPS, depth - 1)), dma((GROUPS, depth - 1)),
-        ],
+        scratch_shapes=scratch,
         compiler_params=pltpu.CompilerParams(
-            collective_id=0, has_side_effects=True, vmem_limit_bytes=60 * 1024 * 1024
+            collective_id=0, has_side_effects=True, vmem_limit_bytes=held + 4 * 1024 * 1024
         ),
         cost_estimate=pl.CostEstimate(
             flops=flops, bytes_accessed=4 * pair_cot.size, transcendentals=0

time: 29.9 us -> 31.2 us (1.043)
  local copies, waits for them, and re-layouts: 1.53 us -> 4.51 us
  Pallas kernels: 27.5 us -> 25.8 us
    unnamed x0 -> x8, local copies, waits for them, and re-layouts: none -> 3.85 us
    pallas_call x1, Pallas kernels: 27.5 us -> 25.8 us  [per_device(): pl.pallas_call(functools.partial(kernel, depth, n_seq, block), out_shape=...]
    squeeze x1, local copies, waits for them, and re-layouts: 1.53 us -> 0.66 us  [per_device(): return (sums[0], sums[1])]
where the time goes in v3:
time: 31.2 us; the launch traced here: 30.9 us
  Pallas kernels  25.8 us (83%)
  local copies, waits for them, and re-layouts  4.51 us (14%)
  between operations  0.65 us (2%)
    pallas_call x1, Pallas kernels, per_device(): pl.pallas_call(functools.partial(kernel, depth, n_seq, block), out_shape=...  25.8 us
    unnamed x8, local copies, waits for them, and re-layouts  3.85 us
    squeeze x1, local copies, waits for them, and re-layouts, per_device(): return (sums[0], sums[1])  0.66 us

profile of v3, /device:TPU:0, one launch (start us, length us, event | category | flops | bytes accessed | tf_op | source)
XLA Modules:
  0.0 30.9 jit_solution(8106776159968603436)
XLA Ops:
  0.6 0.0 copy-start
  0.6 1.2 %copy-done = bf16[16,256,128]{2,1,0:T(8,128)(2,1)S(1)} copy-done((bf16[16,256,128]{2,1,0:T(8,128)(2,1)S(1)}, bf16[16,256,128]{2,1,0:T(8,128)(2,1)}, u32[]{:S(2)}) %copy-start) | copy-done | bytes 1048600
  1.9 0.0 copy-start.1
  1.9 0.9 %copy-done.1 = bf16[1024,128]{1,0:T(8,128)(2,1)S(1)} copy-done((bf16[1024,128]{1,0:T(8,128)(2,1)S(1)}, bf16[1024,128]{1,0:T(8,128)(2,1)}, u32[]{:S(2)}) %copy-start.1) | copy-done | bytes 262168
  2.8 0.0 copy-start.2
  2.8 0.8 %copy-done.2 = bf16[64,512]{1,0:T(8,128)(2,1)S(1)} copy-done((bf16[64,512]{1,0:T(8,128)(2,1)S(1)}, bf16[64,512]{1,0:T(8,128)(2,1)}, u32[]{:S(2)}) %copy-start.2) | copy-done | bytes 65560
  3.6 0.0 copy-start.3
  3.6 0.8 %copy-done.3 = bf16[64,512]{1,0:T(8,128)(2,1)S(1)} copy-done((bf16[64,512]{1,0:T(8,128)(2,1)S(1)}, bf16[64,512]{1,0:T(8,128)(2,1)}, u32[]{:S(2)}) %copy-start.3) | copy-done | bytes 65560
  4.5 25.8 %shard_map.59 = bf16[2,64,512]{2,1,0:T(8,128)(2,1)S(1)} custom-call(bf16[64,512]{1,0:T(8,128)(2,1)S(1)} %copy-done.2, bf16[64,512]{1,0:T(8,128)(2,1)S(1)} %copy-done.3, bf16[16,4,2,2,16,128]{5,4,3,2,1,0:T(8,128)(2,1)S(1)} %bitcast.5, bf16[1024,128]{1,0:T(8,128)(2,1)S(1)} %copy-done.1), custom_call_target="tpu_custom_call" | custom-call | flops 2147483648 | bytes 2097152 | tf_op jit(solution)/shard_map/pallas_call | solution.py:255
  30.3 0.7 %slice_bitcast_fusion = (bf16[64,512]{1,0:T(8,128)(2,1)}, bf16[64,512]{1,0:T(8,128)(2,1)}) fusion(bf16[2,64,512]{2,1,0:T(8,128)(2,1)S(1)} %shard_map.59), kind=kLoop, calls=%fused_computation | loop fusion | bytes 262144 | tf_op jit(solution)/shard_map/squeeze | solution.py:268
Async XLA Ops:
  0.6 1.2 %copy-start = (bf16[16,256,128]{2,1,0:T(8,128)(2,1)S(1)}, bf16[16,256,128]{2,1,0:T(8,128)(2,1)}, u32[]{:S(2)}) copy-start(bf16[16,256,128]{2,1,0:T(8,128)(2,1)} %param.6) | copy-start | bytes 3145732
  1.9 0.9 %copy-start.1 = (bf16[1024,128]{1,0:T(8,128)(2,1)S(1)}, bf16[1024,128]{1,0:T(8,128)(2,1)}, u32[]{:S(2)}) copy-start(bf16[1024,128]{1,0:T(8,128)(2,1)} %weight_ref.1) | copy-start | bytes 786436
  2.8 0.8 %copy-start.2 = (bf16[64,512]{1,0:T(8,128)(2,1)S(1)}, bf16[64,512]{1,0:T(8,128)(2,1)}, u32[]{:S(2)}) copy-start(bf16[64,512]{1,0:T(8,128)(2,1)} %left_ref.1) | copy-start | bytes 196612
  3.6 0.8 %copy-start.3 = (bf16[64,512]{1,0:T(8,128)(2,1)S(1)}, bf16[64,512]{1,0:T(8,128)(2,1)}, u32[]{:S(2)}) copy-start(bf16[64,512]{1,0:T(8,128)(2,1)} %right_ref.1) | copy-start | bytes 196612

commit v4 on v3

--- a/solution.py
+++ b/solution.py
@@ -12,7 +12,7 @@
 CORES = 2
 COLS = 2
 HALF = C // 2
-GROUPS = 2
+GROUPS = 4
 MESH = pl.DeviceIdType.MESH
 F32 = jnp.float32
 BF16 = jnp.bfloat16
@@ -20,8 +20,9 @@
 
 def kernel(
     depth, n_seq, block,
-    left_ref, right_ref, pair_ref, weight_ref,
+    left_hbm, right_hbm, pair_ref, weight_hbm,
     out,
+    left_ref, right_ref, weight_ref,
     pair_own, pair_sib, left_sib, weight_f32, weight_perm, grad, rows_f32,
     gathered, right_all, column_sum, y_send, y_recv, z_send, z_recv,
     left_send, left_recv,
@@ -57,13 +58,29 @@
     for target in [sibling, across] + [at_z(z_peer(d)) for d in range(1, depth)]:
         pl.semaphore_signal(barrier, inc=1, device_id={"row": target}, device_id_type=MESH)
 
-    loads = []
+    load_right = pltpu.make_async_copy(right_hbm, right_ref, load_sem.at[COLS])
+    load_weight = pltpu.make_async_copy(weight_hbm, weight_ref, load_sem.at[COLS + 1])
+    load_left = pltpu.make_async_copy(left_hbm, left_ref, load_sem.at[COLS + 2])
+    loads = [load_left]
     for rel in range(COLS):
         which = col if rel == 0 else 1 - col
         loads.append(pltpu.make_async_copy(
             pair_ref.at[:, :, which, core], pair_own.at[:, rel], load_sem.at[rel]))
-        loads[-1].start()
-
+    for copy in [load_right, load_weight] + loads:
+        copy.start()
+
+    pl.semaphore_wait(barrier, depth + 1)
+
+    sib = []
+    for rel in range(COLS):
+        which = col if rel == 0 else 1 - col
+        sib.append(send(pair_ref.at[:, :, which, 1 - core], pair_sib.at[:, rel],
+                        sib_send.at[rel], sib_recv.at[rel], sibling))
+    sib.append(send(left_hbm, left_sib, sib_send.at[2], sib_recv.at[2], sibling))
+    for copy in sib:
+        copy.start()
+
+    load_right.wait()
     wide = right_ref[...].astype(F32)
     rows_f32[...] = jnp.concatenate([wide, wide], axis=0).T
     low = lax.broadcasted_iota(jnp.int32, (block, lanes), 1) < n_seq
@@ -72,14 +89,6 @@
         odd = rows_f32[pl.ds(2 * ep + 1, block, stride=C), :]
         gathered[ep, 0, z] = jnp.where(low, even, odd).astype(BF16)
 
-    pl.semaphore_wait(barrier, depth + 1)
-
-    sib = []
-    for rel in range(COLS):
-        which = col if rel == 0 else 1 - col
-        sib.append(send(pair_ref.at[:, :, which, 1 - core], pair_sib.at[:, rel],
-                        sib_send.at[rel], sib_recv.at[rel], sibling))
-    sib.append(send(left_ref, left_sib, sib_send.at[2], sib_recv.at[2], sibling))
     gather_z = [
         send(gathered.at[:, 0, z], gathered.at[:, 0, z], agz_send.at[d - 1], agz_recv.at[d - 1],
              at_z(z_peer(d)))
@@ -92,10 +101,9 @@
                              agy_send.at[d], agy_recv.at[d], across))
     for copy in gather_z:
         copy.start()
-    for copy in sib:
-        copy.start()
     gather_y[0].start()
 
+    load_weight.wait()
     weight_f32[...] = weight_ref[...].astype(F32)
     for e in range(C):
         weight_perm[e * C:(e + 1) * C, :] = weight_f32[pl.ds(e, C, stride=C), :].astype(BF16)
@@ -117,7 +125,7 @@
                         res[q * C:(q + 1) * C, k * width:(k + 1) * width])
             return carry
 
-        lax.fori_loop(0, block // 2, step, 0, unroll=2)
+        lax.fori_loop(0, block // 2, step, 0, unroll=4)
 
     reduce_y = [send(y_send.at[g], y_recv.at[g], rsy_send.at[g], rsy_recv.at[g], across)
                 for g in range(GROUPS)]
@@ -161,17 +169,21 @@
 
     for copy in loads:
         copy.wait()
+    for g in range(GROUPS // 2):
+        project(g, pair_own, 0)
+    for copy in sib:
+        copy.wait_recv()
     for g in range(GROUPS):
-        project(g, pair_own, 0)
-        if g == 0:
-            for copy in sib:
-                copy.wait_recv()
+        if g >= GROUPS // 2:
+            project(g, pair_own, 0)
         project(g, pair_sib, chans)
         for d in range(1, depth):
             if (d - 1) * (GROUPS - 1) // (depth - 1) == g - 1:
                 gather_z[d - 1].wait_recv()
                 gather_y[d].start()
         columns(g)
+        if g >= 2:
+            second(g - 2)
 
     for copy in gather_y:
         copy.wait_recv()
@@ -183,11 +195,10 @@
         right_all[2 * ep * width:(2 * ep + 1) * width, :] = piece * mask_even
         right_all[(2 * ep + 1) * width:(2 * ep + 2) * width, :] = piece * mask_odd
 
-    for g in range(GROUPS - 1):
-        second(g)
     left_send[...] = rows(chans)
     exchange = send(left_send, left_recv, sib_send.at[3], sib_recv.at[3], sibling)
     exchange.start()
+    second(GROUPS - 2)
     second(GROUPS - 1)
     mine = rows(0)
     exchange.wait_recv()
@@ -226,6 +237,9 @@
     dma = pltpu.SemaphoreType.DMA
     flops = 2 * block * total * C * C * (p_size + 2 * n_seq)
     scratch = [
+        pltpu.VMEM(left_proj.shape, BF16),
+        pltpu.VMEM(right_proj.shape, BF16),
+        pltpu.VMEM(out_weight.shape, BF16),
         pltpu.VMEM((block, COLS, depth, block, p_size), BF16),
         pltpu.VMEM((block, COLS, depth, block, p_size), BF16),
         pltpu.VMEM((n_seq, chans), BF16),
@@ -242,7 +256,7 @@
         pltpu.VMEM((GROUPS, depth - 1, block, group_lanes), BF16),
         pltpu.VMEM((n_seq, chans), F32),
         pltpu.VMEM((n_seq, chans), F32),
-        dma((COLS,)),
+        dma((COLS + 3,)),
         dma((4,)), dma((4,)),
         dma((depth - 1,)), dma((depth - 1,)),
         dma((depth,)), dma((depth,)),
@@ -251,11 +265,11 @@
     ]
     held = sum(2 * math.prod(b.shape) if b.dtype == BF16 else 4 * math.prod(b.shape)
                for b in scratch if b.dtype in (BF16, F32))
-    held += 2 * 2 * (left_proj.size * 4 + out_weight.size)
+    held += 8 * left_proj.size
     sums = pl.pallas_call(
         functools.partial(kernel, depth, n_seq, block),
-        out_shape=jax.ShapeDtypeStruct((2, n_seq, chans), BF16),
-        in_specs=[vmem, vmem, pl.BlockSpec(memory_space=pltpu.HBM), vmem],
+        out_shape=pltpu.VMEM((2, n_seq, chans), BF16),
+        in_specs=[pl.BlockSpec(memory_space=pltpu.HBM)] * 4,
         out_specs=vmem,
         scratch_shapes=scratch,
         compiler_params=pltpu.CompilerParams(
@@ -264,7 +278,8 @@
         cost_estimate=pl.CostEstimate(
             flops=flops, bytes_accessed=4 * pair_cot.size, transcendentals=0
         ),
-    )(left_proj, right_proj, pair, out_weight)
+    )(*[pltpu.with_memory_space_constraint(x, pltpu.HBM)
+        for x in (left_proj, right_proj, pair, out_weight)])
     return (sums[0], sums[1])
 
 

time: 31.2 us -> 28 us (0.90)
  local copies, waits for them, and re-layouts: 4.51 us -> 0.66 us
  Pallas kernels: 25.8 us -> 26.6 us
    unnamed x8 -> x0, local copies, waits for them, and re-layouts: 3.85 us -> none
    pallas_call x1, Pallas kernels: 25.8 us -> 26.6 us  [per_device(): pl.pallas_call(functools.partial(kernel, depth, n_seq, block), out_shape=...]
where the time goes in v4:
time: 28 us; the launch traced here: 27.9 us
  Pallas kernels  26.6 us (95%)
  local copies, waits for them, and re-layouts  0.66 us (2%)
  between operations  0.64 us (2%)
    pallas_call x1, Pallas kernels, per_device(): pl.pallas_call(functools.partial(kernel, depth, n_seq, block), out_shape=...  26.6 us
    squeeze x1, local copies, waits for them, and re-layouts, per_device(): return (sums[0], sums[1])  0.66 us

profile of v4, /device:TPU:0, one launch (start us, length us, event | category | flops | bytes accessed | tf_op | source)
XLA Modules:
  0.0 27.9 jit_solution(13069465994848015938)
XLA Ops:
  0.6 26.6 %shard_map.59 = bf16[2,64,512]{2,1,0:T(8,128)(2,1)S(1)} custom-call(bf16[64,512]{1,0:T(8,128)(2,1)} %left_hbm.1, bf16[64,512]{1,0:T(8,128)(2,1)} %right_hbm.1, bf16[16,4,2,2,16,128]{5,4,3,2,1,0:T(8,128)(2,1)} %bitcast.5, bf16[1024,128]{1,0:T(8,128)(2,1)} %weight_hbm.1), custom_call_target="tpu_custom_call" | custom-call | flops 2147483648 | bytes 2097152 | tf_op jit(solution)/shard_map/pallas_call | solution.py:269
  27.2 0.7 %slice_bitcast_fusion = (bf16[64,512]{1,0:T(8,128)(2,1)}, bf16[64,512]{1,0:T(8,128)(2,1)}) fusion(bf16[2,64,512]{2,1,0:T(8,128)(2,1)S(1)} %shard_map.59), kind=kLoop, calls=%fused_computation | loop fusion | bytes 262144 | tf_op jit(solution)/shard_map/squeeze | solution.py:283

commit v5 on v4

--- a/solution.py
+++ b/solution.py
@@ -23,7 +23,7 @@
     left_hbm, right_hbm, pair_ref, weight_hbm,
     out,
     left_ref, right_ref, weight_ref,
-    pair_own, pair_sib, left_sib, weight_f32, weight_perm, grad, rows_f32,
+    pair_own, pair_sib, left_sib, weight_f32, weight_perm, grad_a, grad_b, grad_c, grad_d, rows_f32,
     gathered, right_all, column_sum, y_send, y_recv, z_send, z_recv,
     left_send, left_recv,
     load_sem, sib_send, sib_recv, agz_send, agz_recv, agy_send, agy_recv,
@@ -109,6 +109,7 @@
         weight_perm[e * C:(e + 1) * C, :] = weight_f32[pl.ds(e, C, stride=C), :].astype(BF16)
 
     rows_g = C // GROUPS * C
+    grads = (grad_a, grad_b, grad_c, grad_d)
 
     def project(g, pair, first):
         taps = weight_perm[g * rows_g:(g + 1) * rows_g, :]
@@ -118,14 +119,19 @@
             res = lax.dot_general(taps, slab, (((1,), (1,)), ((), ())),
                                   preferred_element_type=F32).astype(BF16)
             for k in range(2):
-                row = pl.multiple_of(first + (2 * t + k) * C, C)
+                row = first + (2 * t + k) * C
+                if not isinstance(t, int):
+                    row = pl.multiple_of(row, C)
                 for q in range(C // GROUPS):
-                    e = g * (C // GROUPS) + q
-                    grad[pl.ds(row, C), e * width:(e + 1) * width] = (
+                    grads[g][pl.ds(row, C), q * width:(q + 1) * width] = (
                         res[q * C:(q + 1) * C, k * width:(k + 1) * width])
             return carry
 
-        lax.fori_loop(0, block // 2, step, 0, unroll=4)
+        if width <= 128:
+            for t in range(block // 2):
+                step(t, 0)
+        else:
+            lax.fori_loop(0, block // 2, step, 0, unroll=2)
 
     reduce_y = [send(y_send.at[g], y_recv.at[g], rsy_send.at[g], rsy_recv.at[g], across)
                 for g in range(GROUPS)]
@@ -137,9 +143,8 @@
     ]
 
     def columns(g):
-        part = slice(g * per_group * 2 * width, (g + 1) * per_group * 2 * width)
-        res = jnp.dot(left_ref[...], grad[:chans, part], preferred_element_type=F32)
-        res += jnp.dot(left_sib[...], grad[chans:, part], preferred_element_type=F32)
+        res = jnp.dot(left_ref[...], grads[g][:chans, :], preferred_element_type=F32)
+        res += jnp.dot(left_sib[...], grads[g][chans:, :], preferred_element_type=F32)
         for q in range(per_group):
             at = 2 * q * width
             turned = jnp.concatenate(
@@ -147,7 +152,6 @@
             where = slice(q * lanes, (q + 1) * lanes)
             column_sum[g, :, where] = turned[:span]
             y_send[g, :, where] = turned[span:].astype(BF16)
-        reduce_y[g].start()
 
     def second(g):
         reduce_y[g].wait_recv()
@@ -161,7 +165,7 @@
         part = per_group * 2 * width
         acc = None
         for g in range(GROUPS):
-            term = jnp.dot(grad[first:first + chans, g * part:(g + 1) * part],
+            term = jnp.dot(grads[g][first:first + chans, :],
                            right_all[g * part:(g + 1) * part, :], preferred_element_type=F32)
             acc = term if acc is None else acc + term
         turned = acc.T
@@ -173,15 +177,18 @@
         project(g, pair_own, 0)
     for copy in sib:
         copy.wait_recv()
+    project(0, pair_sib, chans)
     for g in range(GROUPS):
-        if g >= GROUPS // 2:
-            project(g, pair_own, 0)
-        project(g, pair_sib, chans)
+        if g + 1 < GROUPS:
+            if g + 1 >= GROUPS // 2:
+                project(g + 1, pair_own, 0)
+            project(g + 1, pair_sib, chans)
+        columns(g)
+        reduce_y[g].start()
         for d in range(1, depth):
-            if (d - 1) * (GROUPS - 1) // (depth - 1) == g - 1:
+            if (d - 1) * (GROUPS - 1) // (depth - 1) == g:
                 gather_z[d - 1].wait_recv()
                 gather_y[d].start()
-        columns(g)
         if g >= 2:
             second(g - 2)
 
@@ -245,7 +252,7 @@
         pltpu.VMEM((n_seq, chans), BF16),
         pltpu.VMEM((C * C, p_size), F32),
         pltpu.VMEM((C * C, p_size), BF16),
-        pltpu.VMEM((2 * chans, C * width), BF16),
+        *[pltpu.VMEM((2 * chans, C // GROUPS * width), BF16)] * GROUPS,
         pltpu.VMEM((chans, lanes), F32),
         pltpu.VMEM((HALF, COLS, depth, block, lanes), BF16),
         pltpu.VMEM((C * width, lanes), BF16),

time: 28 us -> 28 us (level)
  no operation moved by 1% of the time
where the time goes in v5:
time: 28 us; the launch traced here: 27.9 us
  Pallas kernels  26.6 us (95%)
  local copies, waits for them, and re-layouts  0.66 us (2%)
  between operations  0.64 us (2%)
    pallas_call x1, Pallas kernels, per_device(): pl.pallas_call(functools.partial(kernel, depth, n_seq, block), out_shape=...  26.6 us
    squeeze x1, local copies, waits for them, and re-layouts, per_device(): return (sums[0], sums[1])  0.66 us

profile of v5, /device:TPU:0, one launch (start us, length us, event | category | flops | bytes accessed | tf_op | source)
XLA Modules:
  0.0 27.9 jit_solution(14776280191763666267)
XLA Ops:
  0.6 26.6 %shard_map.59 = bf16[2,64,512]{2,1,0:T(8,128)(2,1)S(1)} custom-call(bf16[64,512]{1,0:T(8,128)(2,1)} %left_hbm.1, bf16[64,512]{1,0:T(8,128)(2,1)} %right_hbm.1, bf16[16,4,2,2,16,128]{5,4,3,2,1,0:T(8,128)(2,1)} %bitcast.5, bf16[1024,128]{1,0:T(8,128)(2,1)} %weight_hbm.1), custom_call_target="tpu_custom_call" | custom-call | flops 2147483648 | bytes 2097152 | tf_op jit(solution)/shard_map/pallas_call | solution.py:276
  27.2 0.7 %slice_bitcast_fusion = (bf16[64,512]{1,0:T(8,128)(2,1)}, bf16[64,512]{1,0:T(8,128)(2,1)}) fusion(bf16[2,64,512]{2,1,0:T(8,128)(2,1)S(1)} %shard_map.59), kind=kLoop, calls=%fused_computation | loop fusion | bytes 262144 | tf_op jit(solution)/shard_map/squeeze | solution.py:290

commit v6 on v5

--- a/solution.py
+++ b/solution.py
@@ -89,16 +89,24 @@
         odd = rows_f32[pl.ds(2 * ep + 1, block, stride=C), :]
         gathered[ep, 0, z] = jnp.where(low, even, odd).astype(BF16)
 
-    gather_z = [
-        send(gathered.at[:, 0, z], gathered.at[:, 0, z], agz_send.at[d - 1], agz_recv.at[d - 1],
-             at_z(z_peer(d)))
-        for d in range(1, depth)
-    ]
-    gather_y = []
-    for d in range(depth):
-        other = z if d == 0 else lax.rem(z + depth - d, depth)
+    def nearest(k):
+        both = jnp.minimum(z, depth - 1 - z)
+        toward = jnp.where(z < depth - 1 - z, 1, -1)
+        near = z + (k + 1) // 2 * (1 if k % 2 else -1)
+        return jnp.where(k <= 2 * both, near, z + toward * (k - both))
+
+    gather_z = []
+    gather_y = [send(gathered.at[:, 0, z], gathered.at[:, 1, z],
+                     agy_send.at[z], agy_recv.at[z], across)]
+    arrive_z = []
+    for k in range(1, depth):
+        other = nearest(k)
+        gather_z.append(send(gathered.at[:, 0, z], gathered.at[:, 0, z],
+                             agz_send.at[other], agz_recv.at[z], at_z(other)))
+        arrive_z.append(send(gathered.at[:, 0, other], gathered.at[:, 0, other],
+                             agz_send.at[other], agz_recv.at[other], at_z(other)))
         gather_y.append(send(gathered.at[:, 0, other], gathered.at[:, 1, other],
-                             agy_send.at[d], agy_recv.at[d], across))
+                             agy_send.at[other], agy_recv.at[other], across))
     for copy in gather_z:
         copy.start()
     gather_y[0].start()
@@ -186,8 +194,8 @@
         columns(g)
         reduce_y[g].start()
         for d in range(1, depth):
-            if (d - 1) * (GROUPS - 1) // (depth - 1) == g:
-                gather_z[d - 1].wait_recv()
+            if max(1, (2 * d) // (depth - 1)) == g:
+                arrive_z[d - 1].wait_recv()
                 gather_y[d].start()
         if g >= 2:
             second(g - 2)
@@ -265,7 +273,7 @@
         pltpu.VMEM((n_seq, chans), F32),
         dma((COLS + 3,)),
         dma((4,)), dma((4,)),
-        dma((depth - 1,)), dma((depth - 1,)),
+        dma((depth,)), dma((depth,)),
         dma((depth,)), dma((depth,)),
         dma((GROUPS,)), dma((GROUPS,)),
         dma((GROUPS, depth - 1)), dma((GROUPS, depth - 1)),

time: 28 us -> 27.6 us (0.986)
  Pallas kernels: 26.6 us -> 26.1 us
    pallas_call x1, Pallas kernels: 26.6 us -> 26.1 us  [per_device(): pl.pallas_call(functools.partial(kernel, depth, n_seq, block), out_shape=...]
where the time goes in v6:
time: 27.6 us; the launch traced here: 27.4 us
  Pallas kernels  26.1 us (95%)
  local copies, waits for them, and re-layouts  0.66 us (2%)
  between operations  0.64 us (2%)
    pallas_call x1, Pallas kernels, per_device(): pl.pallas_call(functools.partial(kernel, depth, n_seq, block), out_shape=...  26.1 us
    squeeze x1, local copies, waits for them, and re-layouts, per_device(): return (sums[0], sums[1])  0.66 us

profile of v6, /device:TPU:0, one launch (start us, length us, event | category | flops | bytes accessed | tf_op | source)
XLA Modules:
  0.0 27.4 jit_solution(3978665022946593822)
XLA Ops:
  0.6 26.1 %shard_map.59 = bf16[2,64,512]{2,1,0:T(8,128)(2,1)S(1)} custom-call(bf16[64,512]{1,0:T(8,128)(2,1)} %left_hbm.1, bf16[64,512]{1,0:T(8,128)(2,1)} %right_hbm.1, bf16[16,4,2,2,16,128]{5,4,3,2,1,0:T(8,128)(2,1)} %bitcast.5, bf16[1024,128]{1,0:T(8,128)(2,1)} %weight_hbm.1), custom_call_target="tpu_custom_call" | custom-call | flops 2147483648 | bytes 2097152 | tf_op jit(solution)/shard_map/pallas_call | solution.py:284
  26.8 0.7 %slice_bitcast_fusion = (bf16[64,512]{1,0:T(8,128)(2,1)}, bf16[64,512]{1,0:T(8,128)(2,1)}) fusion(bf16[2,64,512]{2,1,0:T(8,128)(2,1)S(1)} %shard_map.59), kind=kLoop, calls=%fused_computation | loop fusion | bytes 262144 | tf_op jit(solution)/shard_map/squeeze | solution.py:298

commit v7 on v6

--- a/solution.py
+++ b/solution.py
@@ -87,7 +87,7 @@
     for ep in range(HALF):
         even = rows_f32[pl.ds(2 * ep, block, stride=C), :]
         odd = rows_f32[pl.ds(2 * ep + 1, block, stride=C), :]
-        gathered[ep, 0, z] = jnp.where(low, even, odd).astype(BF16)
+        gathered[0, z, ep] = jnp.where(low, even, odd).astype(BF16)
 
     def nearest(k):
         both = jnp.minimum(z, depth - 1 - z)
@@ -96,16 +96,16 @@
         return jnp.where(k <= 2 * both, near, z + toward * (k - both))
 
     gather_z = []
-    gather_y = [send(gathered.at[:, 0, z], gathered.at[:, 1, z],
+    gather_y = [send(gathered.at[0, z], gathered.at[1, z],
                      agy_send.at[z], agy_recv.at[z], across)]
     arrive_z = []
     for k in range(1, depth):
         other = nearest(k)
-        gather_z.append(send(gathered.at[:, 0, z], gathered.at[:, 0, z],
+        gather_z.append(send(gathered.at[0, z], gathered.at[0, z],
                              agz_send.at[other], agz_recv.at[z], at_z(other)))
-        arrive_z.append(send(gathered.at[:, 0, other], gathered.at[:, 0, other],
+        arrive_z.append(send(gathered.at[0, other], gathered.at[0, other],
                              agz_send.at[other], agz_recv.at[other], at_z(other)))
-        gather_y.append(send(gathered.at[:, 0, other], gathered.at[:, 1, other],
+        gather_y.append(send(gathered.at[0, other], gathered.at[1, other],
                              agy_send.at[other], agy_recv.at[other], across))
     for copy in gather_z:
         copy.start()
@@ -168,6 +168,17 @@
             z_send[g, k] = column_sum[g, k * block:(k + 1) * block, :].astype(BF16)
         for copy in reduce_z[g]:
             copy.start()
+
+    def finish(g):
+        acc = column_sum[g, pl.ds(pl.multiple_of(z * block, block), block), :]
+        for d in range(1, depth):
+            reduce_z[g][d - 1].wait_recv()
+            acc += z_recv[g, d - 1].astype(F32)
+        for q in range(per_group):
+            ep = g * per_group + q
+            tile = acc[:, q * lanes:(q + 1) * lanes] * (1.0 / n_seq)
+            rows_f32[pl.ds(2 * ep, block, stride=C), :] = tile
+            rows_f32[pl.ds(2 * ep + 1, block, stride=C), :] = pltpu.roll(tile, n_seq, 1)
 
     def rows(first):
         part = per_group * 2 * width
@@ -206,7 +217,7 @@
     mask_odd = upper.astype(F32).astype(BF16)
     mask_even = (1.0 - upper.astype(F32)).astype(BF16)
     for ep in range(HALF):
-        piece = gathered[ep].reshape(width, lanes)
+        piece = gathered[:, :, ep].reshape(width, lanes)
         right_all[2 * ep * width:(2 * ep + 1) * width, :] = piece * mask_even
         right_all[(2 * ep + 1) * width:(2 * ep + 2) * width, :] = piece * mask_odd
 
@@ -215,20 +226,14 @@
     exchange.start()
     second(GROUPS - 2)
     second(GROUPS - 1)
+    for g in range(GROUPS // 2):
+        finish(g)
     mine = rows(0)
     exchange.wait_recv()
     out[0] = ((mine + left_recv[...]) * (1.0 / n_seq)).astype(BF16)
 
-    for g in range(GROUPS):
-        acc = column_sum[g, pl.ds(pl.multiple_of(z * block, block), block), :]
-        for d in range(1, depth):
-            reduce_z[g][d - 1].wait_recv()
-            acc += z_recv[g, d - 1].astype(F32)
-        for q in range(per_group):
-            ep = g * per_group + q
-            tile = acc[:, q * lanes:(q + 1) * lanes] * (1.0 / n_seq)
-            rows_f32[pl.ds(2 * ep, block, stride=C), :] = tile
-            rows_f32[pl.ds(2 * ep + 1, block, stride=C), :] = pltpu.roll(tile, n_seq, 1)
+    for g in range(GROUPS // 2, GROUPS):
+        finish(g)
     out[1] = rows_f32[...].T[:n_seq].astype(BF16)
 
     for copy in sib + gather_z + gather_y + reduce_y + [exchange]:
@@ -262,7 +267,7 @@
         pltpu.VMEM((C * C, p_size), BF16),
         *[pltpu.VMEM((2 * chans, C // GROUPS * width), BF16)] * GROUPS,
         pltpu.VMEM((chans, lanes), F32),
-        pltpu.VMEM((HALF, COLS, depth, block, lanes), BF16),
+        pltpu.VMEM((COLS, depth, HALF, block, lanes), BF16),
         pltpu.VMEM((C * width, lanes), BF16),
         pltpu.VMEM((GROUPS, span, group_lanes), F32),
         pltpu.VMEM((GROUPS, span, group_lanes), BF16),

time: 27.6 us -> 27.6 us (level)
  no operation moved by 1% of the time
where the time goes in v7:
time: 27.6 us; the launch traced here: 27.4 us
  Pallas kernels  26.1 us (95%)
  local copies, waits for them, and re-layouts  0.66 us (2%)
  between operations  0.64 us (2%)
    pallas_call x1, Pallas kernels, per_device(): pl.pallas_call(functools.partial(kernel, depth, n_seq, block), out_shape=...  26.1 us
    squeeze x1, local copies, waits for them, and re-layouts, per_device(): return (sums[0], sums[1])  0.66 us

profile of v7, /device:TPU:0, one launch (start us, length us, event | category | flops | bytes accessed | tf_op | source)
XLA Modules:
  0.0 27.4 jit_solution(5435288287699699109)
XLA Ops:
  0.6 26.1 %shard_map.59 = bf16[2,64,512]{2,1,0:T(8,128)(2,1)S(1)} custom-call(bf16[64,512]{1,0:T(8,128)(2,1)} %left_hbm.1, bf16[64,512]{1,0:T(8,128)(2,1)} %right_hbm.1, bf16[16,4,2,2,16,128]{5,4,3,2,1,0:T(8,128)(2,1)} %bitcast.5, bf16[1024,128]{1,0:T(8,128)(2,1)} %weight_hbm.1), custom_call_target="tpu_custom_call" | custom-call | flops 2147483648 | bytes 2097152 | tf_op jit(solution)/shard_map/pallas_call | solution.py:289
  26.8 0.7 %slice_bitcast_fusion = (bf16[64,512]{1,0:T(8,128)(2,1)}, bf16[64,512]{1,0:T(8,128)(2,1)}) fusion(bf16[2,64,512]{2,1,0:T(8,128)(2,1)S(1)} %shard_map.59), kind=kLoop, calls=%fused_computation | loop fusion | bytes 262144 | tf_op jit(solution)/shard_map/squeeze | solution.py:303

commit v8 on v7

--- a/solution.py
+++ b/solution.py
@@ -116,30 +116,23 @@
     for e in range(C):
         weight_perm[e * C:(e + 1) * C, :] = weight_f32[pl.ds(e, C, stride=C), :].astype(BF16)
 
-    rows_g = C // GROUPS * C
     grads = (grad_a, grad_b, grad_c, grad_d)
-
-    def project(g, pair, first):
-        taps = weight_perm[g * rows_g:(g + 1) * rows_g, :]
-
+    per_grad = C // GROUPS
+
+    def project(pair, first):
         def step(t, carry):
             slab = pair[pl.ds(2 * t, 2)].reshape(2 * width, -1)
-            res = lax.dot_general(taps, slab, (((1,), (1,)), ((), ())),
+            res = lax.dot_general(weight_perm[...], slab, (((1,), (1,)), ((), ())),
                                   preferred_element_type=F32).astype(BF16)
             for k in range(2):
-                row = first + (2 * t + k) * C
-                if not isinstance(t, int):
-                    row = pl.multiple_of(row, C)
-                for q in range(C // GROUPS):
-                    grads[g][pl.ds(row, C), q * width:(q + 1) * width] = (
-                        res[q * C:(q + 1) * C, k * width:(k + 1) * width])
+                row = pl.multiple_of(first + (2 * t + k) * C, C)
+                for e in range(C):
+                    q = e % per_grad
+                    grads[e // per_grad][pl.ds(row, C), q * width:(q + 1) * width] = (
+                        res[e * C:(e + 1) * C, k * width:(k + 1) * width])
             return carry
 
-        if width <= 128:
-            for t in range(block // 2):
-                step(t, 0)
-        else:
-            lax.fori_loop(0, block // 2, step, 0, unroll=2)
+        lax.fori_loop(0, block // 2, step, 0, unroll=2)
 
     reduce_y = [send(y_send.at[g], y_recv.at[g], rsy_send.at[g], rsy_recv.at[g], across)
                 for g in range(GROUPS)]
@@ -192,22 +185,16 @@
 
     for copy in loads:
         copy.wait()
-    for g in range(GROUPS // 2):
-        project(g, pair_own, 0)
+    project(pair_own, 0)
     for copy in sib:
         copy.wait_recv()
-    project(0, pair_sib, chans)
+    project(pair_sib, chans)
+    for k in range(1, depth):
+        arrive_z[k - 1].wait_recv()
+        gather_y[k].start()
     for g in range(GROUPS):
-        if g + 1 < GROUPS:
-            if g + 1 >= GROUPS // 2:
-                project(g + 1, pair_own, 0)
-            project(g + 1, pair_sib, chans)
         columns(g)
         reduce_y[g].start()
-        for d in range(1, depth):
-            if max(1, (2 * d) // (depth - 1)) == g:
-                arrive_z[d - 1].wait_recv()
-                gather_y[d].start()
         if g >= 2:
             second(g - 2)
 

time: 27.6 us -> 28.3 us (1.025)
  Pallas kernels: 26.1 us -> 26.9 us
    pallas_call x1, Pallas kernels: 26.1 us -> 26.9 us  [per_device(): pl.pallas_call(functools.partial(kernel, depth, n_seq, block), out_shape=...]
where the time goes in v8:
time: 28.3 us; the launch traced here: 28.2 us
  Pallas kernels  26.9 us (95%)
  local copies, waits for them, and re-layouts  0.66 us (2%)
  between operations  0.64 us (2%)
    pallas_call x1, Pallas kernels, per_device(): pl.pallas_call(functools.partial(kernel, depth, n_seq, block), out_shape=...  26.9 us
    squeeze x1, local copies, waits for them, and re-layouts, per_device(): return (sums[0], sums[1])  0.66 us

profile of v8, /device:TPU:0, one launch (start us, length us, event | category | flops | bytes accessed | tf_op | source)
XLA Modules:
  0.0 28.2 jit_solution(6765376463937953343)
XLA Ops:
  0.6 26.9 %shard_map.59 = bf16[2,64,512]{2,1,0:T(8,128)(2,1)S(1)} custom-call(bf16[64,512]{1,0:T(8,128)(2,1)} %left_hbm.1, bf16[64,512]{1,0:T(8,128)(2,1)} %right_hbm.1, bf16[16,4,2,2,16,128]{5,4,3,2,1,0:T(8,128)(2,1)} %bitcast.5, bf16[1024,128]{1,0:T(8,128)(2,1)} %weight_hbm.1), custom_call_target="tpu_custom_call" | custom-call | flops 2147483648 | bytes 2097152 | tf_op jit(solution)/shard_map/pallas_call | solution.py:276
  27.5 0.7 %slice_bitcast_fusion = (bf16[64,512]{1,0:T(8,128)(2,1)}, bf16[64,512]{1,0:T(8,128)(2,1)}) fusion(bf16[2,64,512]{2,1,0:T(8,128)(2,1)S(1)} %shard_map.59), kind=kLoop, calls=%fused_computation | loop fusion | bytes 262144 | tf_op jit(solution)/shard_map/squeeze | solution.py:290

commit v9 on v8

--- a/solution.py
+++ b/solution.py
@@ -119,20 +119,22 @@
     grads = (grad_a, grad_b, grad_c, grad_d)
     per_grad = C // GROUPS
 
-    def project(pair, first):
+    def project(pair, first, groups):
+        taps = slice(groups[0] * per_grad * C, (groups[-1] + 1) * per_grad * C)
+
         def step(t, carry):
             slab = pair[pl.ds(2 * t, 2)].reshape(2 * width, -1)
-            res = lax.dot_general(weight_perm[...], slab, (((1,), (1,)), ((), ())),
+            res = lax.dot_general(weight_perm[taps, :], slab, (((1,), (1,)), ((), ())),
                                   preferred_element_type=F32).astype(BF16)
             for k in range(2):
                 row = pl.multiple_of(first + (2 * t + k) * C, C)
-                for e in range(C):
+                for e in range(len(groups) * per_grad):
                     q = e % per_grad
-                    grads[e // per_grad][pl.ds(row, C), q * width:(q + 1) * width] = (
+                    grads[groups[e // per_grad]][pl.ds(row, C), q * width:(q + 1) * width] = (
                         res[e * C:(e + 1) * C, k * width:(k + 1) * width])
             return carry
 
-        lax.fori_loop(0, block // 2, step, 0, unroll=2)
+        lax.fori_loop(0, block // 2, step, 0, unroll=2 if len(groups) > 1 else 4)
 
     reduce_y = [send(y_send.at[g], y_recv.at[g], rsy_send.at[g], rsy_recv.at[g], across)
                 for g in range(GROUPS)]
@@ -185,16 +187,17 @@
 
     for copy in loads:
         copy.wait()
-    project(pair_own, 0)
+    project(pair_own, 0, tuple(range(GROUPS)))
     for copy in sib:
         copy.wait_recv()
-    project(pair_sib, chans)
-    for k in range(1, depth):
-        arrive_z[k - 1].wait_recv()
-        gather_y[k].start()
     for g in range(GROUPS):
+        project(pair_sib, chans, (g,))
         columns(g)
         reduce_y[g].start()
+        for k in range(1, depth):
+            if (2 * (k - 1) + 1) // (depth - 1) == g:
+                arrive_z[k - 1].wait_recv()
+                gather_y[k].start()
         if g >= 2:
             second(g - 2)
 

time: 28.3 us -> 27.2 us (0.961)
  Pallas kernels: 26.9 us -> 25.8 us
    pallas_call x1, Pallas kernels: 26.9 us -> 25.8 us  [per_device(): pl.pallas_call(functools.partial(kernel, depth, n_seq, block), out_shape=...]
where the time goes in v9:
time: 27.2 us; the launch traced here: 27.1 us
  Pallas kernels  25.8 us (95%)
  local copies, waits for them, and re-layouts  0.66 us (2%)
  between operations  0.64 us (2%)
    pallas_call x1, Pallas kernels, per_device(): pl.pallas_call(functools.partial(kernel, depth, n_seq, block), out_shape=...  25.8 us
    squeeze x1, local copies, waits for them, and re-layouts, per_device(): return (sums[0], sums[1])  0.66 us

profile of v9, /device:TPU:0, one launch (start us, length us, event | category | flops | bytes accessed | tf_op | source)
XLA Modules:
  0.0 27.1 jit_solution(11857887713122068542)
XLA Ops:
  0.6 25.8 %shard_map.59 = bf16[2,64,512]{2,1,0:T(8,128)(2,1)S(1)} custom-call(bf16[64,512]{1,0:T(8,128)(2,1)} %left_hbm.1, bf16[64,512]{1,0:T(8,128)(2,1)} %right_hbm.1, bf16[16,4,2,2,16,128]{5,4,3,2,1,0:T(8,128)(2,1)} %bitcast.5, bf16[1024,128]{1,0:T(8,128)(2,1)} %weight_hbm.1), custom_call_target="tpu_custom_call" | custom-call | flops 2147483648 | bytes 2097152 | tf_op jit(solution)/shard_map/pallas_call | solution.py:279
  26.4 0.7 %slice_bitcast_fusion = (bf16[64,512]{1,0:T(8,128)(2,1)}, bf16[64,512]{1,0:T(8,128)(2,1)}) fusion(bf16[2,64,512]{2,1,0:T(8,128)(2,1)S(1)} %shard_map.59), kind=kLoop, calls=%fused_computation | loop fusion | bytes 262144 | tf_op jit(solution)/shard_map/squeeze | solution.py:293

commit v10 on v9

--- a/solution.py
+++ b/solution.py
@@ -69,17 +69,6 @@
     for copy in [load_right, load_weight] + loads:
         copy.start()
 
-    pl.semaphore_wait(barrier, depth + 1)
-
-    sib = []
-    for rel in range(COLS):
-        which = col if rel == 0 else 1 - col
-        sib.append(send(pair_ref.at[:, :, which, 1 - core], pair_sib.at[:, rel],
-                        sib_send.at[rel], sib_recv.at[rel], sibling))
-    sib.append(send(left_hbm, left_sib, sib_send.at[2], sib_recv.at[2], sibling))
-    for copy in sib:
-        copy.start()
-
     load_right.wait()
     wide = right_ref[...].astype(F32)
     rows_f32[...] = jnp.concatenate([wide, wide], axis=0).T
@@ -89,6 +78,14 @@
         odd = rows_f32[pl.ds(2 * ep + 1, block, stride=C), :]
         gathered[0, z, ep] = jnp.where(low, even, odd).astype(BF16)
 
+    pl.semaphore_wait(barrier, depth + 1)
+
+    sib = []
+    for rel in range(COLS):
+        which = col if rel == 0 else 1 - col
+        sib.append(send(pair_ref.at[:, :, which, 1 - core], pair_sib.at[:, rel],
+                        sib_send.at[rel], sib_recv.at[rel], sibling))
+    sib.append(send(left_hbm, left_sib, sib_send.at[2], sib_recv.at[2], sibling))
     def nearest(k):
         both = jnp.minimum(z, depth - 1 - z)
         toward = jnp.where(z < depth - 1 - z, 1, -1)
@@ -110,6 +107,8 @@
     for copy in gather_z:
         copy.start()
     gather_y[0].start()
+    for copy in sib:
+        copy.start()
 
     load_weight.wait()
     weight_f32[...] = weight_ref[...].astype(F32)

time: 27.2 us -> 26.9 us (0.989)
  Pallas kernels: 25.8 us -> 25.5 us
    pallas_call x1, Pallas kernels: 25.8 us -> 25.5 us  [per_device(): pl.pallas_call(functools.partial(kernel, depth, n_seq, block), out_shape=...]
where the time goes in v10:
time: 26.9 us; the launch traced here: 26.8 us
  Pallas kernels  25.5 us (95%)
  local copies, waits for them, and re-layouts  0.66 us (2%)
  between operations  0.64 us (2%)
    pallas_call x1, Pallas kernels, per_device(): pl.pallas_call(functools.partial(kernel, depth, n_seq, block), out_shape=...  25.5 us
    squeeze x1, local copies, waits for them, and re-layouts, per_device(): return (sums[0], sums[1])  0.66 us

profile of v10, /device:TPU:0, one launch (start us, length us, event | category | flops | bytes accessed | tf_op | source)
XLA Modules:
  0.0 26.8 jit_solution(513279766052701568)
XLA Ops:
  0.6 25.5 %shard_map.59 = bf16[2,64,512]{2,1,0:T(8,128)(2,1)S(1)} custom-call(bf16[64,512]{1,0:T(8,128)(2,1)} %left_hbm.1, bf16[64,512]{1,0:T(8,128)(2,1)} %right_hbm.1, bf16[16,4,2,2,16,128]{5,4,3,2,1,0:T(8,128)(2,1)} %bitcast.5, bf16[1024,128]{1,0:T(8,128)(2,1)} %weight_hbm.1), custom_call_target="tpu_custom_call" | custom-call | flops 2147483648 | bytes 2097152 | tf_op jit(solution)/shard_map/pallas_call | solution.py:278
  26.1 0.7 %slice_bitcast_fusion = (bf16[64,512]{1,0:T(8,128)(2,1)}, bf16[64,512]{1,0:T(8,128)(2,1)}) fusion(bf16[2,64,512]{2,1,0:T(8,128)(2,1)S(1)} %shard_map.59), kind=kLoop, calls=%fused_computation | loop fusion | bytes 262144 | tf_op jit(solution)/shard_map/squeeze | solution.py:292

commit v11 on v10

--- a/solution.py
+++ b/solution.py
@@ -194,7 +194,7 @@
         columns(g)
         reduce_y[g].start()
         for k in range(1, depth):
-            if (2 * (k - 1) + 1) // (depth - 1) == g:
+            if max(1, 2 * k // (depth - 1)) == g:
                 arrive_z[k - 1].wait_recv()
                 gather_y[k].start()
         if g >= 2:

time: 26.9 us -> 28.3 us (1.052)
  Pallas kernels: 25.5 us -> 26.9 us
    pallas_call x1, Pallas kernels: 25.5 us -> 26.9 us  [per_device(): pl.pallas_call(functools.partial(kernel, depth, n_seq, block), out_shape=...]
where the time goes in v11:
time: 28.3 us; the launch traced here: 28.2 us
  Pallas kernels  26.9 us (95%)
  local copies, waits for them, and re-layouts  0.66 us (2%)
  between operations  0.64 us (2%)
    pallas_call x1, Pallas kernels, per_device(): pl.pallas_call(functools.partial(kernel, depth, n_seq, block), out_shape=...  26.9 us
    squeeze x1, local copies, waits for them, and re-layouts, per_device(): return (sums[0], sums[1])  0.66 us

profile of v11, /device:TPU:0, one launch (start us, length us, event | category | flops | bytes accessed | tf_op | source)
XLA Modules:
  0.0 28.2 jit_solution(77836008281560244)
XLA Ops:
  0.6 26.9 %shard_map.59 = bf16[2,64,512]{2,1,0:T(8,128)(2,1)S(1)} custom-call(bf16[64,512]{1,0:T(8,128)(2,1)} %left_hbm.1, bf16[64,512]{1,0:T(8,128)(2,1)} %right_hbm.1, bf16[16,4,2,2,16,128]{5,4,3,2,1,0:T(8,128)(2,1)} %bitcast.5, bf16[1024,128]{1,0:T(8,128)(2,1)} %weight_hbm.1), custom_call_target="tpu_custom_call" | custom-call | flops 2147483648 | bytes 2097152 | tf_op jit(solution)/shard_map/pallas_call | solution.py:278
  27.5 0.7 %slice_bitcast_fusion = (bf16[64,512]{1,0:T(8,128)(2,1)}, bf16[64,512]{1,0:T(8,128)(2,1)}) fusion(bf16[2,64,512]{2,1,0:T(8,128)(2,1)S(1)} %shard_map.59), kind=kLoop, calls=%fused_computation | loop fusion | bytes 262144 | tf_op jit(solution)/shard_map/squeeze | solution.py:292

commit v12 on v11

--- a/solution.py
+++ b/solution.py
@@ -194,7 +194,7 @@
         columns(g)
         reduce_y[g].start()
         for k in range(1, depth):
-            if max(1, 2 * k // (depth - 1)) == g:
+            if g == 0:
                 arrive_z[k - 1].wait_recv()
                 gather_y[k].start()
         if g >= 2:

time: 28.3 us -> 27.6 us (0.975)
  Pallas kernels: 26.9 us -> 26.1 us
    pallas_call x1, Pallas kernels: 26.9 us -> 26.1 us  [per_device(): pl.pallas_call(functools.partial(kernel, depth, n_seq, block), out_shape=...]
where the time goes in v12:
time: 27.6 us; the launch traced here: 27.4 us
  Pallas kernels  26.1 us (95%)
  local copies, waits for them, and re-layouts  0.66 us (2%)
  between operations  0.64 us (2%)
    pallas_call x1, Pallas kernels, per_device(): pl.pallas_call(functools.partial(kernel, depth, n_seq, block), out_shape=...  26.1 us
    squeeze x1, local copies, waits for them, and re-layouts, per_device(): return (sums[0], sums[1])  0.66 us

profile of v12, /device:TPU:0, one launch (start us, length us, event | category | flops | bytes accessed | tf_op | source)
XLA Modules:
  0.0 27.4 jit_solution(9714275828186727773)
XLA Ops:
  0.6 26.1 %shard_map.59 = bf16[2,64,512]{2,1,0:T(8,128)(2,1)S(1)} custom-call(bf16[64,512]{1,0:T(8,128)(2,1)} %left_hbm.1, bf16[64,512]{1,0:T(8,128)(2,1)} %right_hbm.1, bf16[16,4,2,2,16,128]{5,4,3,2,1,0:T(8,128)(2,1)} %bitcast.5, bf16[1024,128]{1,0:T(8,128)(2,1)} %weight_hbm.1), custom_call_target="tpu_custom_call" | custom-call | flops 2147483648 | bytes 2097152 | tf_op jit(solution)/shard_map/pallas_call | solution.py:278
  26.7 0.7 %slice_bitcast_fusion = (bf16[64,512]{1,0:T(8,128)(2,1)}, bf16[64,512]{1,0:T(8,128)(2,1)}) fusion(bf16[2,64,512]{2,1,0:T(8,128)(2,1)S(1)} %shard_map.59), kind=kLoop, calls=%fused_computation | loop fusion | bytes 262144 | tf_op jit(solution)/shard_map/squeeze | solution.py:292
